TPU v7x, 32 devices: a whole 2x2x4 slice. The times are simulated.
32 devices in a mesh: dcn: 2 (over core), gx: 4 (over z), gy: 4 (over y, x).
Axes of the slice: x: 2, y: 2, z: 4, core: 2. Of those that a mesh axis runs over, the one named last changes fastest.
Arguments:
- features: bfloat16 [2, 64, 64, 2, 8, 128], P('dcn', 'gx', 'gy'), may hold values from -6 to 6
- grad_out: bfloat16 [2, 64, 64, 2, 8, 128], P('dcn', 'gx', 'gy'), may hold values from -6 to 6
- occupancy: int32 [2, 64, 64, 2, 8], P('dcn', 'gx', 'gy'), may hold values from 0 to 1, as said below
- leaf_z: int32 [2, 8, 8, 2], P('dcn', 'gx', 'gy'), may hold values from -1 to 2, as said below
- neighbours: int32 [2, 8, 8, 2, 27], P('dcn', 'gx', 'gy'), may hold values from 0 to 2, as said below
- kernel: bfloat16 [27, 128, 128], replicated, may hold values from -0.15625 to 0.15625
Outputs:
- grad_features: bfloat16 [2, 64, 64, 2, 8, 128], P('dcn', 'gx', 'gy')
- kernel_grad: float32 [27, 128, 128], replicated
Inputs may be any that keep to these rules, and one draw needn't show every extreme that they name: `leaf_z`: in every leaf column the active slots come first, with distinct z positions in rising order below 3; the other slots hold -1. Every scene has a leaf column with all 2 slots active. `neighbours`: for an active slot holding z position h and offset k = 9 (p + 1) + 3 (q + 1) + (r + 1), the slot of the active leaf at z position h + r in the column p, q away, or 2 if there is none; slots that are not active hold 2 at every offset. `occupancy`: zero at every voxel of a slot that is not active.
All inputs are finite; a program needn't handle non-finite values.
Results may differ from a plain program's by a relative error of at most 0.001.
Values may be sent and summed in bfloat16 or wider, within the bound.
A program may use at most 64 MiB of HBM per device.

v0:
```python
import functools
import math

import jax
import jax.numpy as jnp
from jax import lax
from jax.experimental import pallas as pl
from jax.experimental.pallas import tpu as pltpu
from jax.sharding import PartitionSpec as P

MESH = pl.DeviceIdType.MESH
BF16 = jnp.bfloat16
F32 = jnp.float32


def sides_of(sizes):
    n_gx, n_gy = sizes[1:]
    gx, gy = lax.axis_index("gx"), lax.axis_index("gy")
    sides = []
    for dx in (-1, 0, 1):
        for dy in (-1, 0, 1):
            if dx or dy:
                x, y = gx + dx, gy + dy
                inside = (x >= 0) & (x < n_gx) & (y >= 0) & (y < n_gy)
                sides.append((dx, dy, x, y, inside))
    return sides


def halo_kernel(sizes, cols, leaf_z, grad_out, keep, kernel, dense, wrows, send, recv):
    cols_x, cols_y = cols
    leaves, edge, width = grad_out.shape[2:]
    depth = dense.shape[0]
    voxels = edge * edge * edge
    extent = (cols_x * edge, cols_y * edge)
    dcn = lax.axis_index("dcn")
    sides = sides_of(sizes)
    barrier = pltpu.get_barrier_semaphore()
    for dx, dy, x, y, inside in sides:

        @pl.when(inside)
        def _():
            pl.semaphore_signal(barrier, inc=1, device_id=(dcn, x, y), device_id_type=MESH)

    for cx in range(cols_x):
        for cy in range(cols_y):
            masked = []
            for leaf in range(leaves):
                slot = (cx * cols_y + cy) * leaves + leaf
                cells = grad_out[
                    cx * edge : (cx + 1) * edge, cy * edge : (cy + 1) * edge, leaf
                ].astype(F32)
                kept = jnp.broadcast_to(keep[slot].astype(F32), (width, voxels)).T
                masked.append((leaf_z[cx, cy, leaf], cells * kept.reshape(edge, edge, edge, width)))
            for z in range(depth):
                placed = sum(
                    jnp.where(height == z, cells, jnp.zeros_like(cells))
                    for height, cells in masked
                )
                dense[
                    z,
                    1 + cx * edge : 1 + (cx + 1) * edge,
                    1 + cy * edge : 1 + (cy + 1) * edge,
                ] = placed.astype(BF16)

    def source(step, size):
        return {-1: pl.ds(1, 1), 0: pl.ds(1, size), 1: pl.ds(size, 1)}[step]

    def target(step, size):
        return {-1: pl.ds(size + 1, 1), 0: pl.ds(1, size), 1: pl.ds(0, 1)}[step]

    def copy_to(index):
        dx, dy, x, y, _ = sides[index]
        return pltpu.make_async_remote_copy(
            src_ref=dense.at[:, source(dx, extent[0]), source(dy, extent[1])],
            dst_ref=dense.at[:, target(dx, extent[0]), target(dy, extent[1])],
            send_sem=send.at[index],
            recv_sem=recv.at[index],
            device_id=(dcn, x, y),
            device_id_type=MESH,
        )

    pl.semaphore_wait(barrier, sum(inside.astype(jnp.int32) for *_, inside in sides))

    for index, (dx, dy, x, y, inside) in enumerate(sides):

        @pl.when(inside)
        def _():
            copy_to(index).start()

        @pl.when(jnp.logical_not(inside))
        def _():
            ends = []
            for step, size in ((dx, extent[0]), (dy, extent[1])):
                ends.append({-1: slice(0, 1), 0: slice(1, size + 1), 1: slice(size + 1, size + 2)}[step])
            spot = dense.at[:, ends[0], ends[1]]
            spot[...] = jnp.zeros(spot.shape, BF16)

    for k in range(kernel.shape[0]):
        row, lane = (k % 9) * width, (k // 9) * width
        wrows[row : row + width, lane : lane + width] = kernel[k].astype(F32).T.astype(BF16)

    for index in range(len(sides)):

        @pl.when(sides[index][4])
        def _():
            copy_to(index).wait_send()

        @pl.when(sides[len(sides) - 1 - index][4])
        def _():
            copy_to(index).wait_recv()


def leaf_kernel(cols_y, leaves, leaf_z, dense, own_in, keep, wrows, grad, kacc, patches):
    step = pl.program_id(0)
    edge, width = own_in.shape[3:]
    depth = dense.shape[0]
    wide = edge + 2
    plane = edge * edge
    rows = edge * plane

    @pl.when(step == 0)
    def _():
        kacc[...] = jnp.zeros_like(kacc)

    column = step // leaves
    height = leaf_z[column // cols_y, column % cols_y, step % leaves]
    x0 = (column // cols_y) * edge
    y0 = (column % cols_y) * edge

    @pl.when(height < 0)
    def _():
        grad[...] = jnp.zeros_like(grad)

    @pl.when(height >= 0)
    def _():
        def window(position):
            block = dense[position, pl.ds(x0, wide), pl.ds(y0, wide)]
            return block.astype(F32).reshape(wide * wide, edge, width)

        mid = window(height)
        low = window(jnp.maximum(height - 1, 0))
        low = jnp.where(height > 0, low, jnp.zeros_like(low))
        high = window(jnp.minimum(height + 1, depth - 1))
        high = jnp.where(height < depth - 1, high, jnp.zeros_like(high))
        spot = lax.broadcasted_iota(jnp.int32, low.shape, 1)
        shifted = (
            jnp.where(spot == edge - 1, pltpu.roll(high, edge - 1, 1), pltpu.roll(mid, edge - 1, 1)),
            mid,
            jnp.where(spot == 0, pltpu.roll(low, 1, 1), pltpu.roll(mid, 1, 1)),
        )
        for c in range(3):
            cells = shifted[c].reshape(wide, wide, edge, width)
            for b in range(3):
                piece = cells[:, 2 - b : 2 - b + edge].reshape(wide * plane, width)
                lane = (3 * b + c) * width
                patches[:, lane : lane + width] = piece.astype(BF16)
        kept = jnp.broadcast_to(keep[0].astype(F32), (width, rows))
        own = own_in[:, :, 0].astype(F32).reshape(rows, width)
        own_t = own.T * kept
        gap = jnp.zeros((width, 2 * plane), F32)
        ahead = jnp.concatenate([own_t, gap], axis=1)
        behind = jnp.concatenate([gap, own_t], axis=1)
        shifted_in = jnp.concatenate([behind, pltpu.roll(ahead, plane, 1), ahead], axis=0).astype(BF16)
        terms = jnp.dot(shifted_in, patches[...], preferred_element_type=F32)
        for a in range(3):
            for j in range(9):
                row = (9 * a + j) * width
                kacc[row : row + width, :] += terms[
                    a * width : (a + 1) * width, j * width : (j + 1) * width
                ]
        sums = jnp.dot(patches[...], wrows[...], preferred_element_type=F32)
        result = sum(
            sums[(2 - a) * plane : (2 - a) * plane + rows, a * width : (a + 1) * width]
            for a in range(3)
        )
        result = result * kept.T
        grad[:, :, 0] = result.reshape(edge, edge, edge, width).astype(BF16)


def parts_of(sizes, per):
    blocks = per // 8
    crossed = max(1, int(blocks * 0.36 + 0.5))
    lengths = []
    for total, order in ((blocks - crossed, ("gy", "gx")), (crossed, ("gx", "gy"))):
        lengths.append([((total + 1) // 2, order), (total // 2, order)])
    start = 0
    parts = []
    for pick in (0, 1):
        for choice in lengths:
            length, order = choice[pick]
            if length:
                parts.append((start, 8 * length, order))
                start += 8 * length * sizes[1] * sizes[2]
    return tuple(parts)


def reduce_kernel(sizes, scale, per, acc, out, half_buf, half_sum, *rest):
    n_dcn, n_gx, n_gy = sizes
    parts = parts_of(sizes, per)
    many = len(parts)
    first_buf, first_sum, second_buf = rest[:many], rest[many : 2 * many], rest[2 * many : 3 * many]
    send, recv = rest[3 * many :]
    count = {"dcn": n_dcn, "gx": n_gx, "gy": n_gy}
    here = {name: lax.axis_index(name) for name in count}
    half = per * n_gx * n_gy

    def peer(axis, d):
        return lax.rem(here[axis] + d, count[axis])

    def device(axis, d):
        return tuple(peer(axis, d) if name == axis else here[name] for name in count)

    barrier = pltpu.get_barrier_semaphore()
    others = [(axis, d) for axis in count for d in range(1, count[axis])]
    for axis, d in others:
        pl.semaphore_signal(barrier, inc=1, device_id=device(axis, d), device_id_type=MESH)
    pl.semaphore_wait(barrier, len(others))

    used = [0]

    def copy(src, dst, axis, d):
        slot = used[0]
        used[0] += 1
        made = pltpu.make_async_remote_copy(
            src_ref=src,
            dst_ref=dst,
            send_sem=send.at[slot],
            recv_sem=recv.at[slot],
            device_id=device(axis, d),
            device_id_type=MESH,
        )
        made.start()
        return made

    def span(start, size):
        return pl.ds(pl.multiple_of(start, 8), size)

    def done(copies):
        for made in copies:
            made.wait()

    mine = here["dcn"] * half
    flights = []
    for start, chunk, order in parts:
        size = chunk * n_gx * n_gy
        flights.append(
            [
                copy(
                    acc.at[span(peer("dcn", d) * half + start, size)],
                    half_buf.at[d - 1, span(start, size)],
                    "dcn",
                    d,
                )
                for d in range(1, n_dcn)
            ]
        )
    for i, (start, chunk, order) in enumerate(parts):
        size = chunk * n_gx * n_gy
        done(flights[i])
        total = acc[span(mine + start, size), :]
        for d in range(1, n_dcn):
            total += half_buf[d - 1, span(start, size), :]
        half_sum[span(start, size), :] = total
        piece = size // count[order[0]]
        flights[i] = [
            copy(
                half_sum.at[span(start + peer(order[0], d) * piece, piece)],
                first_buf[i].at[d - 1],
                order[0],
                d,
            )
            for d in range(1, count[order[0]])
        ]
    for i, (start, chunk, order) in enumerate(parts):
        piece = chunk * count[order[1]]
        done(flights[i])
        total = half_sum[span(start + here[order[0]] * piece, piece), :]
        for d in range(1, count[order[0]]):
            total += first_buf[i][d - 1]
        first_sum[i][...] = total
        flights[i] = [
            copy(
                first_sum[i].at[span(peer(order[1], d) * chunk, chunk)],
                second_buf[i].at[d - 1],
                order[1],
                d,
            )
            for d in range(1, count[order[1]])
        ]
    for i, (start, chunk, order) in enumerate(parts):
        piece = chunk * count[order[1]]
        done(flights[i])
        total = first_sum[i][span(here[order[1]] * chunk, chunk), :]
        for d in range(1, count[order[1]]):
            total += second_buf[i][d - 1]
        spot = span(mine + start + here[order[0]] * piece + here[order[1]] * chunk, chunk)
        out[spot, :] = total * scale
        flights[i] = [
            copy(out.at[spot], out.at[spot], order[1], d) for d in range(1, count[order[1]])
        ]
    last = []
    for i, (start, chunk, order) in enumerate(parts):
        piece = chunk * count[order[1]]
        done(flights[i])
        spot = span(mine + start + here[order[0]] * piece, piece)
        flights[i] = [
            copy(out.at[spot], out.at[spot], order[0], d) for d in range(1, count[order[0]])
        ]
        last += [copy(out.at[spot], out.at[spot], "dcn", d) for d in range(1, n_dcn)]
    for i, (start, chunk, order) in enumerate(parts):
        piece = chunk * count[order[1]]
        for d, made in enumerate(flights[i], 1):
            made.wait()
            origin = lax.rem(here[order[0]] + count[order[0]] - d, count[order[0]])
            spot = span(mine + start + origin * piece, piece)
            last += [copy(out.at[spot], out.at[spot], "dcn", e) for e in range(1, n_dcn)]
    done(last)


def local(features, grad_out, occupancy, leaf_z, neighbours, kernel):
    edge = features.shape[4]
    leaves = features.shape[3]
    width = features.shape[-1]
    cols_x = leaf_z.shape[1]
    cols_y = leaf_z.shape[2]
    depth = 3
    voxels = edge * edge * edge
    sizes = tuple(lax.axis_size(name) for name in ("dcn", "gx", "gy"))
    devices = sizes[0] * sizes[1] * sizes[2]
    slots = cols_x * cols_y * leaves
    nx, ny = cols_x * edge, cols_y * edge
    vmem = pl.BlockSpec(memory_space=pltpu.VMEM)
    limit = 40 * 2**20

    heights = leaf_z[0]
    keep = occupancy.reshape(cols_x, edge, cols_y, edge, leaves, edge)
    keep = keep.transpose(0, 2, 4, 1, 3, 5).reshape(slots, 1, voxels)

    dense, wrows = pl.pallas_call(
        functools.partial(halo_kernel, sizes, (cols_x, cols_y)),
        out_shape=[
            jax.ShapeDtypeStruct((depth, nx + 2, ny + 2, edge, width), BF16),
            jax.ShapeDtypeStruct((9 * width, 3 * width), BF16),
        ],
        in_specs=[pl.BlockSpec(memory_space=pltpu.SMEM), vmem, vmem, vmem],
        out_specs=[vmem, vmem],
        scratch_shapes=[pltpu.SemaphoreType.DMA((8,)), pltpu.SemaphoreType.DMA((8,))],
        compiler_params=pltpu.CompilerParams(
            collective_id=0, has_side_effects=True, vmem_limit_bytes=limit
        ),
    )(heights, grad_out[0], keep, kernel)

    per = max(16, -(-27 * width // (devices * 8)) * 8)
    total_rows = per * devices

    def whole(*shape):
        return pl.BlockSpec(shape, lambda i, z: (0,) * len(shape))

    def leaf_at(i, z):
        column = i // leaves
        return (column // cols_y, column % cols_y, i % leaves, 0, 0)

    leaf_block = pl.BlockSpec((edge, edge, 1, edge, width), leaf_at)
    block, kacc = pl.pallas_call(
        functools.partial(leaf_kernel, cols_y, leaves),
        grid_spec=pltpu.PrefetchScalarGridSpec(
            num_scalar_prefetch=1,
            grid=(slots,),
            in_specs=[
                whole(*dense.shape),
                leaf_block,
                pl.BlockSpec((1, 1, voxels), lambda i, z: (i, 0, 0)),
                whole(*wrows.shape),
            ],
            out_specs=[leaf_block, whole(total_rows, width)],
            scratch_shapes=[pltpu.VMEM(((edge + 2) * edge * edge, 9 * width), BF16)],
        ),
        out_shape=[
            jax.ShapeDtypeStruct((nx, ny, leaves, edge, width), BF16),
            jax.ShapeDtypeStruct((total_rows, width), F32),
        ],
        compiler_params=pltpu.CompilerParams(vmem_limit_bytes=limit),
        cost_estimate=pl.CostEstimate(
            flops=4 * slots * voxels * 27 * width * width,
            bytes_accessed=8 * 2**20,
            transcendentals=0,
        ),
    )(heights, dense, features[0], keep, wrows)

    scale = 1.0 / math.sqrt(devices * cols_x * cols_y * voxels * leaves)
    half = total_rows // sizes[0]
    count = {"gx": sizes[1], "gy": sizes[2]}
    parts = parts_of(sizes, per)
    copies = sum(
        sizes[0] - 1 + 2 * (sizes[1] + sizes[2] - 2) + (sizes[0] - 1) * count[order[0]]
        for _, _, order in parts
    )
    kernel_grad = pl.pallas_call(
        functools.partial(reduce_kernel, sizes, scale, per),
        out_shape=jax.ShapeDtypeStruct((total_rows, width), F32),
        in_specs=[vmem],
        out_specs=vmem,
        scratch_shapes=[
            pltpu.VMEM((sizes[0] - 1, half, width), F32),
            pltpu.VMEM((half, width), F32),
        ]
        + [
            pltpu.VMEM((count[order[0]] - 1, chunk * count[order[1]], width), F32)
            for _, chunk, order in parts
        ]
        + [pltpu.VMEM((chunk * count[order[1]], width), F32) for _, chunk, order in parts]
        + [
            pltpu.VMEM((count[order[1]] - 1, chunk, width), F32) for _, chunk, order in parts
        ]
        + [pltpu.SemaphoreType.DMA((copies,)), pltpu.SemaphoreType.DMA((copies,))],
        compiler_params=pltpu.CompilerParams(
            collective_id=1, has_side_effects=True, vmem_limit_bytes=limit
        ),
    )(kacc)
    kernel_grad = kernel_grad[: 27 * width].reshape(27, width, width)
    return (block[None], kernel_grad)


def solution(mesh):
    return jax.shard_map(
        local,
        mesh=mesh,
        in_specs=(
            P("dcn", "gx", "gy", None, None, None),
            P("dcn", "gx", "gy", None, None, None),
            P("dcn", "gx", "gy", None, None),
            P("dcn", "gx", "gy", None),
            P("dcn", "gx", "gy", None, None),
            P(),
        ),
        out_specs=(P("dcn", "gx", "gy", None, None, None), P()),
        check_vma=False,
    )
```

profile of v0, /device:TPU:0, one launch (start us, length us, event | category | flops | bytes accessed | tf_op | source)
XLA Modules:
  0.0 57.8 jit_solution(14748809894026004579)
XLA Ops:
  0.6 0.0 copy-start
  0.6 1.2 %reshape.13 = s32[2,8,2,8,2,8]{3,2,5,4,1,0:T(2,128)S(1)} reshape(s32[1,16,16,2,8]{2,4,3,1,0:T(8,128)} %param.8) | data formatting | bytes 32768 | tf_op jit(solution)/shard_map/reshape | solution.py:336
  1.8 0.1 copy.7
  2.0 0.2 reshape.14.keep
  2.1 0.0 copy-done
  2.2 0.0 copy-start.1
  2.2 1.2 %copy-done.1 = bf16[27,128,128]{2,1,0:T(8,128)(2,1)S(1)} copy-done((bf16[27,128,128]{2,1,0:T(8,128)(2,1)S(1)}, bf16[27,128,128]{2,1,0:T(8,128)(2,1)}, u32[]{:S(2)}) %copy-start.1) | copy-done | bytes 884760
  3.3 0.0 copy-start.2
  3.3 0.7 %copy-done.2 = s32[1,2,2,2]{3,2,1,0:T(2,128)S(1)} copy-done((s32[1,2,2,2]{3,2,1,0:T(2,128)S(1)}, s32[1,2,2,2]{3,2,1,0:T(2,128)}, u32[]{:S(2)}) %copy-start.2) | copy-done | bytes 56
  4.0 0.0 copy-start.3
  4.0 10.0 %shard_map.68 = (bf16[3,18,18,8,128]{4,3,2,1,0:T(8,128)(2,1)S(1)}, bf16[1152,384]{1,0:T(8,128)(2,1)S(1)}) custom-call(s32[2,2,2]{2,1,0:T(2,128)S(1)} %bitcast.13, bf16[16,16,2,8,128]{4,3,2,1,0:T(8,128)(2,1)S(1)} %bitcast.12, s32[8,1,512]{2,1,0:T(1,128)S(1)} %reshape.14.keep, bf16[27,128,128]{2,1,0:T(8,128)(2,1)S(1)} %copy-done.1), custom_call_target="tpu_custom_call" | custom-call | tf_op jit(solution)/shard_map/pallas_call | solution.py:339
  14.0 0.0 copy-done.3
  14.0 12.0 %shard_map.69 = (bf16[16,16,2,8,128]{4,3,2,1,0:T(8,128)(2,1)}, f32[3584,128]{1,0:T(8,128)S(1)}) custom-call(s32[2,2,2]{2,1,0:T(2,128)S(1)} %bitcast.14, bf16[3,18,18,8,128]{4,3,2,1,0:T(8,128)(2,1)S(1)} %get-tuple-element.6.dense, bf16[16,16,2,8,128]{4,3,2,1,0:T(8,128)(2,1)S(1)} %bitcast.15, s32[8,1,512]{2,1,0:T(1,128)S(1)} %reshape.14.keep, ...), custom_call_target="tpu_custom_call" | custom-call | flops 7247757312 | bytes 8388608 | tf_op jit(solution)/shard_map/pallas_call | solution.py:364
  26.0 30.5 %shard_map.70 = f32[3584,128]{1,0:T(8,128)S(1)} custom-call(f32[3584,128]{1,0:T(8,128)S(1)} %get-tuple-element.9.acc), custom_call_target="tpu_custom_call" | custom-call | tf_op jit(solution)/shard_map/pallas_call | solution.py:398
  56.5 1.3 %slice.3 = f32[3456,128]{1,0:T(8,128)} slice(f32[3584,128]{1,0:T(8,128)S(1)} %shard_map.70), slice={[0:3456], [0:128]} | slice | bytes 3538944 | tf_op jit(solution)/shard_map/slice | solution.py:420
Async XLA Ops:
  0.6 1.5 %copy-start = (bf16[1,16,16,2,8,128]{5,4,3,2,1,0:T(8,128)(2,1)S(1)}, bf16[1,16,16,2,8,128]{5,4,3,2,1,0:T(8,128)(2,1)}, u32[]{:S(2)}) copy-start(bf16[1,16,16,2,8,128]{5,4,3,2,1,0:T(8,128)(2,1)} %param.7) | copy-start | bytes 3145732
  2.2 1.2 %copy-start.1 = (bf16[27,128,128]{2,1,0:T(8,128)(2,1)S(1)}, bf16[27,128,128]{2,1,0:T(8,128)(2,1)}, u32[]{:S(2)}) copy-start(bf16[27,128,128]{2,1,0:T(8,128)(2,1)} %kernel.1) | copy-start | bytes 2654212
  3.3 0.7 %copy-start.2 = (s32[1,2,2,2]{3,2,1,0:T(2,128)S(1)}, s32[1,2,2,2]{3,2,1,0:T(2,128)}, u32[]{:S(2)}) copy-start(s32[1,2,2,2]{3,2,1,0:T(2,128)} %param.9) | copy-start | bytes 100
  4.0 10.0 %copy-start.3 = (bf16[1,16,16,2,8,128]{5,4,3,2,1,0:T(8,128)(2,1)S(1)}, bf16[1,16,16,2,8,128]{5,4,3,2,1,0:T(8,128)(2,1)}, u32[]{:S(2)}) copy-start(bf16[1,16,16,2,8,128]{5,4,3,2,1,0:T(8,128)(2,1)} %param.6) | copy-start | bytes 3145732
where the time goes:
time: 58.6 us; the launch traced here: 57.8 us
  Pallas kernels  52.5 us (90%)
  local copies, waits for them, and re-layouts  4.66 us (8%)
  between operations  0.7 us (1%)
    pallas_call x1, Pallas kernels, local(): pl.pallas_call(functools.partial(reduce_kernel, sizes, scale, per), out_s...  30.5 us
    pallas_call x1, Pallas kernels, local(): pl.pallas_call(functools.partial(leaf_kernel, cols_y, leaves), grid_spec=...  12 us
    pallas_call x1, Pallas kernels, local(): pl.pallas_call(functools.partial(halo_kernel, sizes, (cols_x, cols_y)), o...  9.98 us
    unnamed x8, local copies, waits for them, and re-layouts  1.85 us
    slice x1, local copies, waits for them, and re-layouts, local(): kernel_grad = kernel_grad[:27 * width].reshape(27, width, width)  1.32 us
    reshape x2, local copies, waits for them, and re-layouts, local(): keep = occupancy.reshape(cols_x, edge, cols_y, edge, leaves, edge)  1.32 us

commit v1 on v0

--- a/solution.py
+++ b/solution.py
@@ -26,7 +26,9 @@
     return sides
 
 
-def halo_kernel(sizes, cols, leaf_z, grad_out, keep, kernel, dense, wrows, send, recv):
+def halo_kernel(
+    sizes, cols, leaf_z, keep, grad_far, kernel_far, dense, wrows, grad_out, kernel, near, send, recv
+):
     cols_x, cols_y = cols
     leaves, edge, width = grad_out.shape[2:]
     depth = dense.shape[0]
@@ -34,6 +36,10 @@
     extent = (cols_x * edge, cols_y * edge)
     dcn = lax.axis_index("dcn")
     sides = sides_of(sizes)
+    fetch_grad = pltpu.make_async_copy(grad_far, grad_out, near.at[0])
+    fetch_kernel = pltpu.make_async_copy(kernel_far, kernel, near.at[1])
+    fetch_grad.start()
+    fetch_kernel.start()
     barrier = pltpu.get_barrier_semaphore()
     for dx, dy, x, y, inside in sides:
 
@@ -41,6 +47,7 @@
         def _():
             pl.semaphore_signal(barrier, inc=1, device_id=(dcn, x, y), device_id_type=MESH)
 
+    fetch_grad.wait()
     for cx in range(cols_x):
         for cy in range(cols_y):
             masked = []
@@ -95,9 +102,9 @@
             spot = dense.at[:, ends[0], ends[1]]
             spot[...] = jnp.zeros(spot.shape, BF16)
 
+    fetch_kernel.wait()
     for k in range(kernel.shape[0]):
-        row, lane = (k % 9) * width, (k // 9) * width
-        wrows[row : row + width, lane : lane + width] = kernel[k].astype(F32).T.astype(BF16)
+        wrows[k * width : (k + 1) * width, :] = kernel[k].astype(F32).T.astype(BF16)
 
     for index in range(len(sides)):
 
@@ -110,71 +117,67 @@
             copy_to(index).wait_recv()
 
 
-def leaf_kernel(cols_y, leaves, leaf_z, dense, own_in, keep, wrows, grad, kacc, patches):
-    step = pl.program_id(0)
-    edge, width = own_in.shape[3:]
+def leaf_kernel(leaf_z, dense, features, keep, wrows, grad, kacc, patches):
+    cols_x, cols_y, leaves = leaf_z.shape
+    edge, width = features.shape[3:]
     depth = dense.shape[0]
     wide = edge + 2
     plane = edge * edge
     rows = edge * plane
-
-    @pl.when(step == 0)
-    def _():
-        kacc[...] = jnp.zeros_like(kacc)
-
-    column = step // leaves
-    height = leaf_z[column // cols_y, column % cols_y, step % leaves]
-    x0 = (column // cols_y) * edge
-    y0 = (column % cols_y) * edge
-
-    @pl.when(height < 0)
-    def _():
-        grad[...] = jnp.zeros_like(grad)
-
-    @pl.when(height >= 0)
-    def _():
-        def window(position):
-            block = dense[position, pl.ds(x0, wide), pl.ds(y0, wide)]
-            return block.astype(F32).reshape(wide * wide, edge, width)
-
-        mid = window(height)
-        low = window(jnp.maximum(height - 1, 0))
-        low = jnp.where(height > 0, low, jnp.zeros_like(low))
-        high = window(jnp.minimum(height + 1, depth - 1))
-        high = jnp.where(height < depth - 1, high, jnp.zeros_like(high))
-        spot = lax.broadcasted_iota(jnp.int32, low.shape, 1)
-        shifted = (
-            jnp.where(spot == edge - 1, pltpu.roll(high, edge - 1, 1), pltpu.roll(mid, edge - 1, 1)),
-            mid,
-            jnp.where(spot == 0, pltpu.roll(low, 1, 1), pltpu.roll(mid, 1, 1)),
-        )
-        for c in range(3):
-            cells = shifted[c].reshape(wide, wide, edge, width)
-            for b in range(3):
-                piece = cells[:, 2 - b : 2 - b + edge].reshape(wide * plane, width)
-                lane = (3 * b + c) * width
-                patches[:, lane : lane + width] = piece.astype(BF16)
-        kept = jnp.broadcast_to(keep[0].astype(F32), (width, rows))
-        own = own_in[:, :, 0].astype(F32).reshape(rows, width)
-        own_t = own.T * kept
-        gap = jnp.zeros((width, 2 * plane), F32)
-        ahead = jnp.concatenate([own_t, gap], axis=1)
-        behind = jnp.concatenate([gap, own_t], axis=1)
-        shifted_in = jnp.concatenate([behind, pltpu.roll(ahead, plane, 1), ahead], axis=0).astype(BF16)
-        terms = jnp.dot(shifted_in, patches[...], preferred_element_type=F32)
-        for a in range(3):
-            for j in range(9):
-                row = (9 * a + j) * width
-                kacc[row : row + width, :] += terms[
-                    a * width : (a + 1) * width, j * width : (j + 1) * width
-                ]
-        sums = jnp.dot(patches[...], wrows[...], preferred_element_type=F32)
-        result = sum(
-            sums[(2 - a) * plane : (2 - a) * plane + rows, a * width : (a + 1) * width]
-            for a in range(3)
-        )
-        result = result * kept.T
-        grad[:, :, 0] = result.reshape(edge, edge, edge, width).astype(BF16)
+    kacc[...] = jnp.zeros_like(kacc)
+
+    @pl.loop(0, cols_x * cols_y * leaves)
+    def _(slot):
+        column, leaf = slot // leaves, slot % leaves
+        cx, cy = column // cols_y, column % cols_y
+        height = leaf_z[cx, cy, leaf]
+        x0, y0 = cx * edge, cy * edge
+
+        @pl.when(height < 0)
+        def _():
+            grad[pl.ds(x0, edge), pl.ds(y0, edge), leaf] = jnp.zeros((edge, edge, edge, width), BF16)
+
+        @pl.when(height >= 0)
+        def _():
+            def window(position):
+                block = dense[position, pl.ds(x0, wide), pl.ds(y0, wide)]
+                return block.astype(F32).reshape(wide * wide, edge, width)
+
+            mid = window(height)
+            low = window(jnp.maximum(height - 1, 0))
+            low = jnp.where(height > 0, low, jnp.zeros_like(low))
+            high = window(jnp.minimum(height + 1, depth - 1))
+            high = jnp.where(height < depth - 1, high, jnp.zeros_like(high))
+            spot = lax.broadcasted_iota(jnp.int32, low.shape, 1)
+            last = edge - 1
+            shifted = (
+                jnp.where(spot == last, pltpu.roll(high, last, 1), pltpu.roll(mid, last, 1)),
+                mid,
+                jnp.where(spot == 0, pltpu.roll(low, 1, 1), pltpu.roll(mid, 1, 1)),
+            )
+            for c in range(3):
+                cells = shifted[c].reshape(wide, wide, edge, width)
+                for b in range(3):
+                    piece = cells[:, 2 - b : 2 - b + edge].reshape(wide * plane, width)
+                    lane = (3 * b + c) * width
+                    patches[:, lane : lane + width] = piece.astype(BF16)
+            kept = jnp.broadcast_to(keep[slot].astype(F32), (width, rows))
+            own = features[pl.ds(x0, edge), pl.ds(y0, edge), leaf].astype(F32)
+            own_t = (own.reshape(rows, width).T * kept).astype(BF16)
+            result = jnp.zeros((rows, width), F32)
+            for a in range(3):
+                columns = patches[(2 - a) * plane : (2 - a) * plane + rows, :]
+                result += jnp.dot(
+                    columns,
+                    wrows[9 * a * width : 9 * (a + 1) * width, :],
+                    preferred_element_type=F32,
+                )
+                terms = jnp.dot(own_t, columns, preferred_element_type=F32)
+                for j in range(9):
+                    row = (9 * a + j) * width
+                    kacc[row : row + width, :] += terms[:, j * width : (j + 1) * width]
+            result = (result * kept.T).reshape(edge, edge, edge, width)
+            grad[pl.ds(x0, edge), pl.ds(y0, edge), leaf] = result.astype(BF16)
 
 
 def parts_of(sizes, per):
@@ -330,6 +333,8 @@
     slots = cols_x * cols_y * leaves
     nx, ny = cols_x * edge, cols_y * edge
     vmem = pl.BlockSpec(memory_space=pltpu.VMEM)
+    smem = pl.BlockSpec(memory_space=pltpu.SMEM)
+    far = pl.BlockSpec(memory_space=pltpu.HBM)
     limit = 40 * 2**20
 
     heights = leaf_z[0]
@@ -340,41 +345,30 @@
         functools.partial(halo_kernel, sizes, (cols_x, cols_y)),
         out_shape=[
             jax.ShapeDtypeStruct((depth, nx + 2, ny + 2, edge, width), BF16),
-            jax.ShapeDtypeStruct((9 * width, 3 * width), BF16),
+            jax.ShapeDtypeStruct((27 * width, width), BF16),
         ],
-        in_specs=[pl.BlockSpec(memory_space=pltpu.SMEM), vmem, vmem, vmem],
+        in_specs=[smem, vmem, far, far],
         out_specs=[vmem, vmem],
-        scratch_shapes=[pltpu.SemaphoreType.DMA((8,)), pltpu.SemaphoreType.DMA((8,))],
+        scratch_shapes=[
+            pltpu.VMEM((nx, ny, leaves, edge, width), BF16),
+            pltpu.VMEM(kernel.shape, BF16),
+            pltpu.SemaphoreType.DMA((2,)),
+            pltpu.SemaphoreType.DMA((8,)),
+            pltpu.SemaphoreType.DMA((8,)),
+        ],
         compiler_params=pltpu.CompilerParams(
             collective_id=0, has_side_effects=True, vmem_limit_bytes=limit
         ),
-    )(heights, grad_out[0], keep, kernel)
+    )(heights, keep, grad_out[0], kernel)
 
     per = max(16, -(-27 * width // (devices * 8)) * 8)
     total_rows = per * devices
 
-    def whole(*shape):
-        return pl.BlockSpec(shape, lambda i, z: (0,) * len(shape))
-
-    def leaf_at(i, z):
-        column = i // leaves
-        return (column // cols_y, column % cols_y, i % leaves, 0, 0)
-
-    leaf_block = pl.BlockSpec((edge, edge, 1, edge, width), leaf_at)
     block, kacc = pl.pallas_call(
-        functools.partial(leaf_kernel, cols_y, leaves),
-        grid_spec=pltpu.PrefetchScalarGridSpec(
-            num_scalar_prefetch=1,
-            grid=(slots,),
-            in_specs=[
-                whole(*dense.shape),
-                leaf_block,
-                pl.BlockSpec((1, 1, voxels), lambda i, z: (i, 0, 0)),
-                whole(*wrows.shape),
-            ],
-            out_specs=[leaf_block, whole(total_rows, width)],
-            scratch_shapes=[pltpu.VMEM(((edge + 2) * edge * edge, 9 * width), BF16)],
-        ),
+        leaf_kernel,
+        in_specs=[smem, vmem, vmem, vmem, vmem],
+        out_specs=[vmem, vmem],
+        scratch_shapes=[pltpu.VMEM(((edge + 2) * edge * edge, 9 * width), BF16)],
         out_shape=[
             jax.ShapeDtypeStruct((nx, ny, leaves, edge, width), BF16),
             jax.ShapeDtypeStruct((total_rows, width), F32),

time: 58.6 us -> 56.9 us (0.971)
  Pallas kernels: 52.5 us -> 51.1 us
    pallas_call x1, Pallas kernels: 12 us -> 9.28 us  [local(): pl.pallas_call(leaf_kernel, in_specs=[smem, vmem, vmem, vmem, vmem], out_...]
    pallas_call x1, Pallas kernels: 30.5 us -> 31.5 us  [local(): pl.pallas_call(functools.partial(reduce_kernel, sizes, scale, per), out_s...]
where the time goes in v1:
time: 56.9 us; the launch traced here: 56.4 us
  Pallas kernels  51.1 us (90%)
  local copies, waits for them, and re-layouts  4.66 us (8%)
  between operations  0.7 us (1%)
    pallas_call x1, Pallas kernels, local(): pl.pallas_call(functools.partial(reduce_kernel, sizes, scale, per), out_s...  31.5 us
    pallas_call x1, Pallas kernels, local(): pl.pallas_call(functools.partial(halo_kernel, sizes, (cols_x, cols_y)), o...  10.3 us
    pallas_call x1, Pallas kernels, local(): pl.pallas_call(leaf_kernel, in_specs=[smem, vmem, vmem, vmem, vmem], out_...  9.28 us
    unnamed x8, local copies, waits for them, and re-layouts  1.85 us
    slice x1, local copies, waits for them, and re-layouts, local(): kernel_grad = kernel_grad[:27 * width].reshape(27, width, width)  1.32 us
    reshape x2, local copies, waits for them, and re-layouts, local(): keep = occupancy.reshape(cols_x, edge, cols_y, edge, leaves, edge)  1.32 us

profile of v1, /device:TPU:0, one launch (start us, length us, event | category | flops | bytes accessed | tf_op | source)
XLA Modules:
  0.0 56.4 jit_solution(2248642530142663179)
XLA Ops:
  0.6 0.0 copy-start
  0.6 1.2 %reshape.13 = s32[2,8,2,8,2,8]{3,2,5,4,1,0:T(2,128)S(1)} reshape(s32[1,16,16,2,8]{2,4,3,1,0:T(8,128)} %param.8) | data formatting | bytes 32768 | tf_op jit(solution)/shard_map/reshape | solution.py:341
  1.8 0.1 copy.7
  2.0 0.2 reshape.14.keep
  2.1 0.0 copy-done
  2.2 0.0 copy-start.1
  2.2 1.2 %copy-done.1 = bf16[27,128,128]{2,1,0:T(8,128)(2,1)S(1)} copy-done((bf16[27,128,128]{2,1,0:T(8,128)(2,1)S(1)}, bf16[27,128,128]{2,1,0:T(8,128)(2,1)}, u32[]{:S(2)}) %copy-start.1) | copy-done | bytes 884760
  3.3 0.0 copy-start.2
  3.3 0.7 %copy-done.2 = s32[1,2,2,2]{3,2,1,0:T(2,128)S(1)} copy-done((s32[1,2,2,2]{3,2,1,0:T(2,128)S(1)}, s32[1,2,2,2]{3,2,1,0:T(2,128)}, u32[]{:S(2)}) %copy-start.2) | copy-done | bytes 56
  4.0 0.0 copy-start.3
  4.0 10.3 %shard_map.68 = (bf16[3,18,18,8,128]{4,3,2,1,0:T(8,128)(2,1)S(1)}, bf16[3456,128]{1,0:T(8,128)(2,1)S(1)}) custom-call(s32[2,2,2]{2,1,0:T(2,128)S(1)} %bitcast.13, s32[8,1,512]{2,1,0:T(1,128)S(1)} %reshape.14.keep, bf16[16,16,2,8,128]{4,3,2,1,0:T(8,128)(2,1)S(1)} %bitcast.12, bf16[27,128,128]{2,1,0:T(8,128)(2,1)S(1)} %copy-done.1), custom_call_target="tpu_custom_call" | custom-call | tf_op jit(solution)/shard_map/pallas_call | solution.py:344
  14.3 0.0 copy-done.3
  14.3 9.3 %shard_map.69 = (bf16[16,16,2,8,128]{4,3,2,1,0:T(8,128)(2,1)}, f32[3584,128]{1,0:T(8,128)S(1)}) custom-call(s32[2,2,2]{2,1,0:T(2,128)S(1)} %bitcast.14, bf16[3,18,18,8,128]{4,3,2,1,0:T(8,128)(2,1)S(1)} %get-tuple-element.6.dense, bf16[16,16,2,8,128]{4,3,2,1,0:T(8,128)(2,1)S(1)} %bitcast.15, s32[8,1,512]{2,1,0:T(1,128)S(1)} %reshape.14.keep, ...), custom_call_target="tpu_custom_call" | custom-call | flops 7247757312 | bytes 8388608 | tf_op jit(solution)/shard_map/pallas_call | solution.py:367
  23.6 31.5 %shard_map.70 = f32[3584,128]{1,0:T(8,128)S(1)} custom-call(f32[3584,128]{1,0:T(8,128)S(1)} %get-tuple-element.9.acc), custom_call_target="tpu_custom_call" | custom-call | tf_op jit(solution)/shard_map/pallas_call | solution.py:392
  55.1 1.3 %slice.3 = f32[3456,128]{1,0:T(8,128)} slice(f32[3584,128]{1,0:T(8,128)S(1)} %shard_map.70), slice={[0:3456], [0:128]} | slice | bytes 3538944 | tf_op jit(solution)/shard_map/slice | solution.py:414
Async XLA Ops:
  0.6 1.5 %copy-start = (bf16[1,16,16,2,8,128]{5,4,3,2,1,0:T(8,128)(2,1)S(1)}, bf16[1,16,16,2,8,128]{5,4,3,2,1,0:T(8,128)(2,1)}, u32[]{:S(2)}) copy-start(bf16[1,16,16,2,8,128]{5,4,3,2,1,0:T(8,128)(2,1)} %param.7) | copy-start | bytes 3145732
  2.2 1.2 %copy-start.1 = (bf16[27,128,128]{2,1,0:T(8,128)(2,1)S(1)}, bf16[27,128,128]{2,1,0:T(8,128)(2,1)}, u32[]{:S(2)}) copy-start(bf16[27,128,128]{2,1,0:T(8,128)(2,1)} %kernel_far.1) | copy-start | bytes 2654212
  3.3 0.7 %copy-start.2 = (s32[1,2,2,2]{3,2,1,0:T(2,128)S(1)}, s32[1,2,2,2]{3,2,1,0:T(2,128)}, u32[]{:S(2)}) copy-start(s32[1,2,2,2]{3,2,1,0:T(2,128)} %param.9) | copy-start | bytes 100
  4.0 10.3 %copy-start.3 = (bf16[1,16,16,2,8,128]{5,4,3,2,1,0:T(8,128)(2,1)S(1)}, bf16[1,16,16,2,8,128]{5,4,3,2,1,0:T(8,128)(2,1)}, u32[]{:S(2)}) copy-start(bf16[1,16,16,2,8,128]{5,4,3,2,1,0:T(8,128)(2,1)} %param.6) | copy-start | bytes 3145732

commit v2 on v1

--- a/solution.py
+++ b/solution.py
@@ -184,7 +184,7 @@
     blocks = per // 8
     crossed = max(1, int(blocks * 0.36 + 0.5))
     lengths = []
-    for total, order in ((blocks - crossed, ("gy", "gx")), (crossed, ("gx", "gy"))):
+    for total, order in ((blocks - crossed, ("gy", "low", "high")), (crossed, ("low", "high", "gy"))):
         lengths.append([((total + 1) // 2, order), (total // 2, order)])
     start = 0
     parts = []
@@ -197,21 +197,33 @@
     return tuple(parts)
 
 
-def reduce_kernel(sizes, scale, per, acc, out, half_buf, half_sum, *rest):
-    n_dcn, n_gx, n_gy = sizes
+def counts_of(sizes):
+    low = 2 if sizes[1] % 2 == 0 else 1
+    return {"dcn": sizes[0], "gy": sizes[2], "low": low, "high": sizes[1] // low}
+
+
+def reduce_kernel(sizes, scale, per, acc, out, half_buf, *rest):
+    count = counts_of(sizes)
+    gx = lax.axis_index("gx")
+    here = {
+        "dcn": lax.axis_index("dcn"),
+        "gy": lax.axis_index("gy"),
+        "low": lax.rem(gx, count["low"]),
+        "high": gx // count["low"],
+    }
+    half = per * sizes[1] * sizes[2]
     parts = parts_of(sizes, per)
-    many = len(parts)
-    first_buf, first_sum, second_buf = rest[:many], rest[many : 2 * many], rest[2 * many : 3 * many]
-    send, recv = rest[3 * many :]
-    count = {"dcn": n_dcn, "gx": n_gx, "gy": n_gy}
-    here = {name: lax.axis_index(name) for name in count}
-    half = per * n_gx * n_gy
+    many = 3 * len(parts)
+    bufs, sums = rest[:many], rest[many : 2 * many]
+    send, recv = rest[2 * many :]
 
     def peer(axis, d):
         return lax.rem(here[axis] + d, count[axis])
 
     def device(axis, d):
-        return tuple(peer(axis, d) if name == axis else here[name] for name in count)
+        at = dict(here)
+        at[axis] = peer(axis, d)
+        return (at["dcn"], at["high"] * count["low"] + at["low"], at["gy"])
 
     barrier = pltpu.get_barrier_semaphore()
     others = [(axis, d) for axis in count for d in range(1, count[axis])]
@@ -244,8 +256,13 @@
 
     mine = here["dcn"] * half
     flights = []
+    lengths = []
     for start, chunk, order in parts:
-        size = chunk * n_gx * n_gy
+        size = chunk * sizes[1] * sizes[2]
+        steps = [size]
+        for axis in order:
+            steps.append(steps[-1] // count[axis])
+        lengths.append(steps)
         flights.append(
             [
                 copy(
@@ -254,69 +271,66 @@
                     "dcn",
                     d,
                 )
-                for d in range(1, n_dcn)
+                for d in range(1, count["dcn"])
             ]
         )
+    for stage in range(4):
+        for i, (start, chunk, order) in enumerate(parts):
+            size = lengths[i][stage]
+            done(flights[i])
+            if stage == 0:
+                total = acc[span(mine + start, size), :]
+                for d in range(1, count["dcn"]):
+                    total += half_buf[d - 1, span(start, size), :]
+            else:
+                axis = order[stage - 1]
+                total = sums[3 * i + stage - 1][span(here[axis] * size, size), :]
+                for d in range(1, count[axis]):
+                    total += bufs[3 * i + stage - 1][d - 1]
+            if stage < 3:
+                axis, piece = order[stage], lengths[i][stage + 1]
+                held = sums[3 * i + stage]
+                held[...] = total
+                flights[i] = [
+                    copy(
+                        held.at[span(peer(axis, d) * piece, piece)],
+                        bufs[3 * i + stage].at[d - 1],
+                        axis,
+                        d,
+                    )
+                    for d in range(1, count[axis])
+                ]
+            else:
+                spot = mine + start
+                for axis, length in zip(order, lengths[i][1:]):
+                    spot += here[axis] * length
+                spot = span(spot, size)
+                out[spot, :] = total * scale
+                flights[i] = [
+                    copy(out.at[spot], out.at[spot], order[2], d)
+                    for d in range(1, count[order[2]])
+                ]
+    last = []
+    for stage in (1, 0):
+        for i, (start, chunk, order) in enumerate(parts):
+            done(flights[i])
+            spot = mine + start
+            for axis, length in zip(order[: stage + 1], lengths[i][1:]):
+                spot += here[axis] * length
+            spot = span(spot, lengths[i][stage + 1])
+            axis = order[stage]
+            flights[i] = [
+                copy(out.at[spot], out.at[spot], axis, d) for d in range(1, count[axis])
+            ]
+            if stage == 0:
+                last += [copy(out.at[spot], out.at[spot], "dcn", d) for d in range(1, count["dcn"])]
     for i, (start, chunk, order) in enumerate(parts):
-        size = chunk * n_gx * n_gy
-        done(flights[i])
-        total = acc[span(mine + start, size), :]
-        for d in range(1, n_dcn):
-            total += half_buf[d - 1, span(start, size), :]
-        half_sum[span(start, size), :] = total
-        piece = size // count[order[0]]
-        flights[i] = [
-            copy(
-                half_sum.at[span(start + peer(order[0], d) * piece, piece)],
-                first_buf[i].at[d - 1],
-                order[0],
-                d,
-            )
-            for d in range(1, count[order[0]])
-        ]
-    for i, (start, chunk, order) in enumerate(parts):
-        piece = chunk * count[order[1]]
-        done(flights[i])
-        total = half_sum[span(start + here[order[0]] * piece, piece), :]
-        for d in range(1, count[order[0]]):
-            total += first_buf[i][d - 1]
-        first_sum[i][...] = total
-        flights[i] = [
-            copy(
-                first_sum[i].at[span(peer(order[1], d) * chunk, chunk)],
-                second_buf[i].at[d - 1],
-                order[1],
-                d,
-            )
-            for d in range(1, count[order[1]])
-        ]
-    for i, (start, chunk, order) in enumerate(parts):
-        piece = chunk * count[order[1]]
-        done(flights[i])
-        total = first_sum[i][span(here[order[1]] * chunk, chunk), :]
-        for d in range(1, count[order[1]]):
-            total += second_buf[i][d - 1]
-        spot = span(mine + start + here[order[0]] * piece + here[order[1]] * chunk, chunk)
-        out[spot, :] = total * scale
-        flights[i] = [
-            copy(out.at[spot], out.at[spot], order[1], d) for d in range(1, count[order[1]])
-        ]
-    last = []
-    for i, (start, chunk, order) in enumerate(parts):
-        piece = chunk * count[order[1]]
-        done(flights[i])
-        spot = span(mine + start + here[order[0]] * piece, piece)
-        flights[i] = [
-            copy(out.at[spot], out.at[spot], order[0], d) for d in range(1, count[order[0]])
-        ]
-        last += [copy(out.at[spot], out.at[spot], "dcn", d) for d in range(1, n_dcn)]
-    for i, (start, chunk, order) in enumerate(parts):
-        piece = chunk * count[order[1]]
+        axis, piece = order[0], lengths[i][1]
         for d, made in enumerate(flights[i], 1):
             made.wait()
-            origin = lax.rem(here[order[0]] + count[order[0]] - d, count[order[0]])
+            origin = lax.rem(here[axis] + count[axis] - d, count[axis])
             spot = span(mine + start + origin * piece, piece)
-            last += [copy(out.at[spot], out.at[spot], "dcn", e) for e in range(1, n_dcn)]
+            last += [copy(out.at[spot], out.at[spot], "dcn", e) for e in range(1, count["dcn"])]
     done(last)
 
 
@@ -383,12 +397,17 @@
 
     scale = 1.0 / math.sqrt(devices * cols_x * cols_y * voxels * leaves)
     half = total_rows // sizes[0]
-    count = {"gx": sizes[1], "gy": sizes[2]}
-    parts = parts_of(sizes, per)
-    copies = sum(
-        sizes[0] - 1 + 2 * (sizes[1] + sizes[2] - 2) + (sizes[0] - 1) * count[order[0]]
-        for _, _, order in parts
-    )
+    count = counts_of(sizes)
+    copies = 0
+    bufs, sums = [], []
+    for _, chunk, order in parts_of(sizes, per):
+        size = chunk * sizes[1] * sizes[2]
+        for axis in order:
+            sums.append(pltpu.VMEM((size, width), F32))
+            size //= count[axis]
+            bufs.append(pltpu.VMEM((max(1, count[axis] - 1), size, width), F32))
+            copies += 2 * (count[axis] - 1)
+        copies += (sizes[0] - 1) * (1 + count[order[0]])
     kernel_grad = pl.pallas_call(
         functools.partial(reduce_kernel, sizes, scale, per),
         out_shape=jax.ShapeDtypeStruct((total_rows, width), F32),
@@ -396,16 +415,9 @@
         out_specs=vmem,
         scratch_shapes=[
             pltpu.VMEM((sizes[0] - 1, half, width), F32),
-            pltpu.VMEM((half, width), F32),
         ]
-        + [
-            pltpu.VMEM((count[order[0]] - 1, chunk * count[order[1]], width), F32)
-            for _, chunk, order in parts
-        ]
-        + [pltpu.VMEM((chunk * count[order[1]], width), F32) for _, chunk, order in parts]
-        + [
-            pltpu.VMEM((count[order[1]] - 1, chunk, width), F32) for _, chunk, order in parts
-        ]
+        + bufs
+        + sums
         + [pltpu.SemaphoreType.DMA((copies,)), pltpu.SemaphoreType.DMA((copies,))],
         compiler_params=pltpu.CompilerParams(
             collective_id=1, has_side_effects=True, vmem_limit_bytes=limit

time: 56.9 us -> 60.3 us (1.060); the launches traced: 56.4 us -> 60.6 us
  Pallas kernels: 51.1 us -> 55.2 us
    pallas_call x1, Pallas kernels: 31.5 us -> 35.7 us  [local(): pl.pallas_call(functools.partial(reduce_kernel, sizes, scale, per), out_s...]
where the time goes in v2:
time: 60.3 us; the launch traced here: 60.6 us
  Pallas kernels  55.2 us (92%)
  local copies, waits for them, and re-layouts  4.66 us (8%)
  between operations  0.7 us (1%)
    pallas_call x1, Pallas kernels, local(): pl.pallas_call(functools.partial(reduce_kernel, sizes, scale, per), out_s...  35.7 us
    pallas_call x1, Pallas kernels, local(): pl.pallas_call(functools.partial(halo_kernel, sizes, (cols_x, cols_y)), o...  10.3 us
    pallas_call x1, Pallas kernels, local(): pl.pallas_call(leaf_kernel, in_specs=[smem, vmem, vmem, vmem, vmem], out_...  9.29 us
    unnamed x8, local copies, waits for them, and re-layouts  1.85 us
    slice x1, local copies, waits for them, and re-layouts, local(): kernel_grad = kernel_grad[:27 * width].reshape(27, width, width)  1.32 us
    reshape x2, local copies, waits for them, and re-layouts, local(): keep = occupancy.reshape(cols_x, edge, cols_y, edge, leaves, edge)  1.32 us

profile of v2, /device:TPU:0, one launch (start us, length us, event | category | flops | bytes accessed | tf_op | source)
XLA Modules:
  0.0 60.6 jit_solution(14659793129479775204)
XLA Ops:
  0.6 0.0 copy-start
  0.6 1.2 %reshape.13 = s32[2,8,2,8,2,8]{3,2,5,4,1,0:T(2,128)S(1)} reshape(s32[1,16,16,2,8]{2,4,3,1,0:T(8,128)} %param.8) | data formatting | bytes 32768 | tf_op jit(solution)/shard_map/reshape | solution.py:355
  1.8 0.1 copy.7
  2.0 0.2 reshape.14.keep
  2.1 0.0 copy-done
  2.2 0.0 copy-start.1
  2.2 1.2 %copy-done.1 = bf16[27,128,128]{2,1,0:T(8,128)(2,1)S(1)} copy-done((bf16[27,128,128]{2,1,0:T(8,128)(2,1)S(1)}, bf16[27,128,128]{2,1,0:T(8,128)(2,1)}, u32[]{:S(2)}) %copy-start.1) | copy-done | bytes 884760
  3.3 0.0 copy-start.2
  3.3 0.7 %copy-done.2 = s32[1,2,2,2]{3,2,1,0:T(2,128)S(1)} copy-done((s32[1,2,2,2]{3,2,1,0:T(2,128)S(1)}, s32[1,2,2,2]{3,2,1,0:T(2,128)}, u32[]{:S(2)}) %copy-start.2) | copy-done | bytes 56
  4.0 0.0 copy-start.3
  4.0 10.3 %shard_map.68 = (bf16[3,18,18,8,128]{4,3,2,1,0:T(8,128)(2,1)S(1)}, bf16[3456,128]{1,0:T(8,128)(2,1)S(1)}) custom-call(s32[2,2,2]{2,1,0:T(2,128)S(1)} %bitcast.13, s32[8,1,512]{2,1,0:T(1,128)S(1)} %reshape.14.keep, bf16[16,16,2,8,128]{4,3,2,1,0:T(8,128)(2,1)S(1)} %bitcast.12, bf16[27,128,128]{2,1,0:T(8,128)(2,1)S(1)} %copy-done.1), custom_call_target="tpu_custom_call" | custom-call | tf_op jit(solution)/shard_map/pallas_call | solution.py:358
  14.3 0.0 copy-done.3
  14.3 9.3 %shard_map.69 = (bf16[16,16,2,8,128]{4,3,2,1,0:T(8,128)(2,1)}, f32[3584,128]{1,0:T(8,128)S(1)}) custom-call(s32[2,2,2]{2,1,0:T(2,128)S(1)} %bitcast.14, bf16[3,18,18,8,128]{4,3,2,1,0:T(8,128)(2,1)S(1)} %get-tuple-element.6.dense, bf16[16,16,2,8,128]{4,3,2,1,0:T(8,128)(2,1)S(1)} %bitcast.15, s32[8,1,512]{2,1,0:T(1,128)S(1)} %reshape.14.keep, ...), custom_call_target="tpu_custom_call" | custom-call | flops 7247757312 | bytes 8388608 | tf_op jit(solution)/shard_map/pallas_call | solution.py:381
  23.6 35.7 %shard_map.70 = f32[3584,128]{1,0:T(8,128)S(1)} custom-call(f32[3584,128]{1,0:T(8,128)S(1)} %get-tuple-element.9.acc), custom_call_target="tpu_custom_call" | custom-call | tf_op jit(solution)/shard_map/pallas_call | solution.py:411
  59.3 1.3 %slice.3 = f32[3456,128]{1,0:T(8,128)} slice(f32[3584,128]{1,0:T(8,128)S(1)} %shard_map.70), slice={[0:3456], [0:128]} | slice | bytes 3538944 | tf_op jit(solution)/shard_map/slice | solution.py:426
Async XLA Ops:
  0.6 1.5 %copy-start = (bf16[1,16,16,2,8,128]{5,4,3,2,1,0:T(8,128)(2,1)S(1)}, bf16[1,16,16,2,8,128]{5,4,3,2,1,0:T(8,128)(2,1)}, u32[]{:S(2)}) copy-start(bf16[1,16,16,2,8,128]{5,4,3,2,1,0:T(8,128)(2,1)} %param.7) | copy-start | bytes 3145732
  2.2 1.2 %copy-start.1 = (bf16[27,128,128]{2,1,0:T(8,128)(2,1)S(1)}, bf16[27,128,128]{2,1,0:T(8,128)(2,1)}, u32[]{:S(2)}) copy-start(bf16[27,128,128]{2,1,0:T(8,128)(2,1)} %kernel_far.1) | copy-start | bytes 2654212
  3.3 0.7 %copy-start.2 = (s32[1,2,2,2]{3,2,1,0:T(2,128)S(1)}, s32[1,2,2,2]{3,2,1,0:T(2,128)}, u32[]{:S(2)}) copy-start(s32[1,2,2,2]{3,2,1,0:T(2,128)} %param.9) | copy-start | bytes 100
  4.0 10.3 %copy-start.3 = (bf16[1,16,16,2,8,128]{5,4,3,2,1,0:T(8,128)(2,1)S(1)}, bf16[1,16,16,2,8,128]{5,4,3,2,1,0:T(8,128)(2,1)}, u32[]{:S(2)}) copy-start(bf16[1,16,16,2,8,128]{5,4,3,2,1,0:T(8,128)(2,1)} %param.6) | copy-start | bytes 3145732

commit v3 on v1

--- a/solution.py
+++ b/solution.py
@@ -27,7 +27,7 @@
 
 
 def halo_kernel(
-    sizes, cols, leaf_z, keep, grad_far, kernel_far, dense, wrows, grad_out, kernel, near, send, recv
+    sizes, cols, leaf_z, keep, grad_far, dense, grad_out, near, send, recv
 ):
     cols_x, cols_y = cols
     leaves, edge, width = grad_out.shape[2:]
@@ -37,9 +37,7 @@
     dcn = lax.axis_index("dcn")
     sides = sides_of(sizes)
     fetch_grad = pltpu.make_async_copy(grad_far, grad_out, near.at[0])
-    fetch_kernel = pltpu.make_async_copy(kernel_far, kernel, near.at[1])
     fetch_grad.start()
-    fetch_kernel.start()
     barrier = pltpu.get_barrier_semaphore()
     for dx, dy, x, y, inside in sides:
 
@@ -102,10 +100,6 @@
             spot = dense.at[:, ends[0], ends[1]]
             spot[...] = jnp.zeros(spot.shape, BF16)
 
-    fetch_kernel.wait()
-    for k in range(kernel.shape[0]):
-        wrows[k * width : (k + 1) * width, :] = kernel[k].astype(F32).T.astype(BF16)
-
     for index in range(len(sides)):
 
         @pl.when(sides[index][4])
@@ -117,7 +111,7 @@
             copy_to(index).wait_recv()
 
 
-def leaf_kernel(leaf_z, dense, features, keep, wrows, grad, kacc, patches):
+def leaf_kernel(leaf_z, dense, features, keep, kernel, grad, kacc, patches, wrows):
     cols_x, cols_y, leaves = leaf_z.shape
     edge, width = features.shape[3:]
     depth = dense.shape[0]
@@ -125,6 +119,8 @@
     plane = edge * edge
     rows = edge * plane
     kacc[...] = jnp.zeros_like(kacc)
+    for k in range(kernel.shape[0]):
+        wrows[k * width : (k + 1) * width, :] = kernel[k].astype(F32).T.astype(BF16)
 
     @pl.loop(0, cols_x * cols_y * leaves)
     def _(slot):
@@ -182,7 +178,7 @@
 
 def parts_of(sizes, per):
     blocks = per // 8
-    crossed = max(1, int(blocks * 0.36 + 0.5))
+    crossed = max(1, int(blocks * 0.29 + 0.5))
     lengths = []
     for total, order in ((blocks - crossed, ("gy", "gx")), (crossed, ("gx", "gy"))):
         lengths.append([((total + 1) // 2, order), (total // 2, order)])
@@ -341,25 +337,21 @@
     keep = occupancy.reshape(cols_x, edge, cols_y, edge, leaves, edge)
     keep = keep.transpose(0, 2, 4, 1, 3, 5).reshape(slots, 1, voxels)
 
-    dense, wrows = pl.pallas_call(
+    dense = pl.pallas_call(
         functools.partial(halo_kernel, sizes, (cols_x, cols_y)),
-        out_shape=[
-            jax.ShapeDtypeStruct((depth, nx + 2, ny + 2, edge, width), BF16),
-            jax.ShapeDtypeStruct((27 * width, width), BF16),
-        ],
-        in_specs=[smem, vmem, far, far],
-        out_specs=[vmem, vmem],
+        out_shape=jax.ShapeDtypeStruct((depth, nx + 2, ny + 2, edge, width), BF16),
+        in_specs=[smem, vmem, far],
+        out_specs=vmem,
         scratch_shapes=[
             pltpu.VMEM((nx, ny, leaves, edge, width), BF16),
-            pltpu.VMEM(kernel.shape, BF16),
-            pltpu.SemaphoreType.DMA((2,)),
+            pltpu.SemaphoreType.DMA((1,)),
             pltpu.SemaphoreType.DMA((8,)),
             pltpu.SemaphoreType.DMA((8,)),
         ],
         compiler_params=pltpu.CompilerParams(
             collective_id=0, has_side_effects=True, vmem_limit_bytes=limit
         ),
-    )(heights, keep, grad_out[0], kernel)
+    )(heights, keep, grad_out[0])
 
     per = max(16, -(-27 * width // (devices * 8)) * 8)
     total_rows = per * devices
@@ -368,7 +360,10 @@
         leaf_kernel,
         in_specs=[smem, vmem, vmem, vmem, vmem],
         out_specs=[vmem, vmem],
-        scratch_shapes=[pltpu.VMEM(((edge + 2) * edge * edge, 9 * width), BF16)],
+        scratch_shapes=[
+            pltpu.VMEM(((edge + 2) * edge * edge, 9 * width), BF16),
+            pltpu.VMEM((27 * width, width), BF16),
+        ],
         out_shape=[
             jax.ShapeDtypeStruct((nx, ny, leaves, edge, width), BF16),
             jax.ShapeDtypeStruct((total_rows, width), F32),
@@ -379,7 +374,7 @@
             bytes_accessed=8 * 2**20,
             transcendentals=0,
         ),
-    )(heights, dense, features[0], keep, wrows)
+    )(heights, dense, features[0], keep, kernel)
 
     scale = 1.0 / math.sqrt(devices * cols_x * cols_y * voxels * leaves)
     half = total_rows // sizes[0]

time: 56.9 us -> 55.9 us (0.982); the launches traced: 56.4 us -> 56.1 us
  local copies, waits for them, and re-layouts: 4.66 us -> 3.49 us
  Pallas kernels: 51.1 us -> 51.9 us
    unnamed x8, local copies, waits for them, and re-layouts: 1.85 us -> 0.69 us
    pallas_call x1, Pallas kernels: 31.5 us -> 32.3 us  [local(): pl.pallas_call(functools.partial(reduce_kernel, sizes, scale, per), out_s...]
where the time goes in v3:
time: 55.9 us; the launch traced here: 56.1 us
  Pallas kernels  51.9 us (93%)
  local copies, waits for them, and re-layouts  3.49 us (6%)
  between operations  0.71 us (1%)
    pallas_call x1, Pallas kernels, local(): pl.pallas_call(functools.partial(reduce_kernel, sizes, scale, per), out_s...  32.3 us
    pallas_call x1, Pallas kernels, local(): pl.pallas_call(functools.partial(halo_kernel, sizes, (cols_x, cols_y)), o...  10.1 us
    pallas_call x1, Pallas kernels, local(): pl.pallas_call(leaf_kernel, in_specs=[smem, vmem, vmem, vmem, vmem], out_...  9.51 us
    slice x1, local copies, waits for them, and re-layouts, local(): kernel_grad = kernel_grad[:27 * width].reshape(27, width, width)  1.32 us
    reshape x2, local copies, waits for them, and re-layouts, local(): keep = occupancy.reshape(cols_x, edge, cols_y, edge, leaves, edge)  1.32 us

profile of v3, /device:TPU:0, one launch (start us, length us, event | category | flops | bytes accessed | tf_op | source)
XLA Modules:
  0.0 56.1 jit_solution(7276595860463586515)
XLA Ops:
  0.6 0.0 copy-start
  0.6 1.2 %reshape.13 = s32[2,8,2,8,2,8]{3,2,5,4,1,0:T(2,128)S(1)} reshape(s32[1,16,16,2,8]{2,4,3,1,0:T(8,128)} %param.8) | data formatting | bytes 32768 | tf_op jit(solution)/shard_map/reshape | solution.py:337
  1.8 0.1 copy.7
  2.0 0.2 reshape.14.keep
  2.1 0.0 copy-done
  2.2 0.0 copy-start.1
  2.2 0.7 %copy-done.1 = s32[1,2,2,2]{3,2,1,0:T(2,128)S(1)} copy-done((s32[1,2,2,2]{3,2,1,0:T(2,128)S(1)}, s32[1,2,2,2]{3,2,1,0:T(2,128)}, u32[]{:S(2)}) %copy-start.1) | copy-done | bytes 56
  2.8 0.0 copy-start.2
  2.8 0.0 copy-start.3
  2.8 10.1 %shard_map.68.dense = bf16[3,18,18,8,128]{4,3,2,1,0:T(8,128)(2,1)S(1)} custom-call(s32[2,2,2]{2,1,0:T(2,128)S(1)} %bitcast.13, s32[8,1,512]{2,1,0:T(1,128)S(1)} %reshape.14.keep, bf16[16,16,2,8,128]{4,3,2,1,0:T(8,128)(2,1)S(1)} %bitcast.12), custom_call_target="tpu_custom_call" | custom-call | tf_op jit(solution)/shard_map/pallas_call | solution.py:340
  12.9 0.0 copy-done.2
  12.9 0.0 copy-done.3
  12.9 9.5 %shard_map.69 = (bf16[16,16,2,8,128]{4,3,2,1,0:T(8,128)(2,1)}, f32[3584,128]{1,0:T(8,128)S(1)}) custom-call(s32[2,2,2]{2,1,0:T(2,128)S(1)} %bitcast.14, bf16[3,18,18,8,128]{4,3,2,1,0:T(8,128)(2,1)S(1)} %shard_map.68.dense, bf16[16,16,2,8,128]{4,3,2,1,0:T(8,128)(2,1)S(1)} %bitcast.15, s32[8,1,512]{2,1,0:T(1,128)S(1)} %reshape.14.keep, ...), custom_call_target="tpu_custom_call" | custom-call | flops 7247757312 | bytes 8388608 | tf_op jit(solution)/shard_map/pallas_call | solution.py:359
  22.5 32.3 %shard_map.70 = f32[3584,128]{1,0:T(8,128)S(1)} custom-call(f32[3584,128]{1,0:T(8,128)S(1)} %get-tuple-element.5.acc), custom_call_target="tpu_custom_call" | custom-call | tf_op jit(solution)/shard_map/pallas_call | solution.py:387
  54.8 1.3 %slice.3 = f32[3456,128]{1,0:T(8,128)} slice(f32[3584,128]{1,0:T(8,128)S(1)} %shard_map.70), slice={[0:3456], [0:128]} | slice | bytes 3538944 | tf_op jit(solution)/shard_map/slice | solution.py:409
Async XLA Ops:
  0.6 1.5 %copy-start = (bf16[1,16,16,2,8,128]{5,4,3,2,1,0:T(8,128)(2,1)S(1)}, bf16[1,16,16,2,8,128]{5,4,3,2,1,0:T(8,128)(2,1)}, u32[]{:S(2)}) copy-start(bf16[1,16,16,2,8,128]{5,4,3,2,1,0:T(8,128)(2,1)} %param.7) | copy-start | bytes 3145732
  2.2 0.7 %copy-start.1 = (s32[1,2,2,2]{3,2,1,0:T(2,128)S(1)}, s32[1,2,2,2]{3,2,1,0:T(2,128)}, u32[]{:S(2)}) copy-start(s32[1,2,2,2]{3,2,1,0:T(2,128)} %param.9) | copy-start | bytes 100
  2.8 10.1 %copy-start.2 = (bf16[1,16,16,2,8,128]{5,4,3,2,1,0:T(8,128)(2,1)S(1)}, bf16[1,16,16,2,8,128]{5,4,3,2,1,0:T(8,128)(2,1)}, u32[]{:S(2)}) copy-start(bf16[1,16,16,2,8,128]{5,4,3,2,1,0:T(8,128)(2,1)} %param.6) | copy-start | bytes 3145732
  2.8 10.1 %copy-start.3 = (bf16[27,128,128]{2,1,0:T(8,128)(2,1)S(1)}, bf16[27,128,128]{2,1,0:T(8,128)(2,1)}, u32[]{:S(2)}) copy-start(bf16[27,128,128]{2,1,0:T(8,128)(2,1)} %kernel.1) | copy-start | bytes 2654212
